TPU v7x, 32 devices: a whole 2x2x4 slice. The times are simulated.
32 devices in a mesh: groups: 2 (over x), gx: 16 (over z, y, core).
Axes of the slice: x: 2, y: 2, z: 4, core: 2. Of those that a mesh axis runs over, the one named last changes fastest.
Arguments:
- adjoint_state: float32 [8, 96, 128, 128], P(None, 'groups', 'gx'), parts along dimension 1, may hold values from -6 to 6
- forward_fields: bfloat16 [2, 3, 96, 128, 128], P(None, None, 'groups', 'gx'), parts along dimension 2, may hold values from -6 to 6
- vel_coeffs: float32 [8, 128], P('groups'), parts along dimension 0, may hold values from 0.2 to 0.8
- stress_coeffs: float32 [8, 128], P('groups'), parts along dimension 0, may hold values from 0.15 to 0.6
- drm_cells: int32 [4096], P('gx'), may hold values from 120 to 16383, as said below
- drm_force: float32 [32, 2, 2, 4096], P('groups', None, None, 'gx'), parts along dimension 0, may hold values from -6 to 6
- source_id: int32 [96], P('groups'), parts along dimension 0, may hold values from 0 to 15
Outputs:
- adjoint_out: float32 [8, 96, 128, 128], P(None, 'groups', 'gx'), parts along dimension 1
- gradients: float32 [4, 128], P('groups'), parts along dimension 0
There are 2 independent parts, one for each index of `groups`. A program takes and returns all parts, laid end to end along the dimension named above; an argument that names none is the same for every part. Nothing has to cross between parts.
Inputs may be any that keep to these rules, and one draw needn't show every extreme that they name: `drm_cells`: in each aligned block b of 256 entries, every entry names a cell x * 128 + z with b * 8 <= x < (b + 1) * 8 and 120 <= z < 128; cells may repeat.
All inputs are finite; a program needn't handle non-finite values.
Results may differ from a plain program's by a relative error of at most 0.0003.
Values sent between devices are 32-bit elements; how exact they have to be, the bound alone decides.
A program may use at most 64 MiB of HBM per device.

v0:
```python
import functools

import jax
import jax.numpy as jnp
from jax import lax
from jax.experimental import pallas as pl
from jax.experimental.pallas import tpu as pltpu
from jax.sharding import PartitionSpec as P

CHUNKS = 2
VX, VZ, QX, QZ, XX, ZZ, XZ, PR = range(8)


def sum_stages(n):
    near = 4 if n % 4 == 0 else 1
    return [(1, n)]


def coeff_rows(coeffs):
    return [coeffs[i : i + 1] for i in range(4)]


def depth_lower(values, lane):
    return values - jnp.where(lane == 0, 0.0, pltpu.roll(values, 1, 1))


def depth_upper(values, lane):
    last = values.shape[1] - 1
    return jnp.where(lane == last, 0.0, pltpu.roll(values, last, 1)) - values


def velocity(fields, sides, vel, lane, forcing=None):
    vel_x, vel_z, flow_x, flow_z, _, stress_zz, stress_xz, pressure = fields
    solid, couple, fluid, drag = vel
    force_x = sides[0] + depth_lower(stress_xz, lane)
    force_z = sides[1] + depth_lower(stress_zz, lane)
    push_x = sides[2] + drag * flow_x
    push_z = depth_lower(pressure, lane) + drag * flow_z
    new_x = vel_x + solid * force_x + couple * push_x
    new_z = vel_z + solid * force_z + couple * push_z
    if forcing is not None:
        new_x = new_x + forcing[0]
        new_z = new_z + forcing[1]
    flow_x = flow_x - couple * force_x - fluid * push_x
    flow_z = flow_z - couple * force_z - fluid * push_z
    return [new_x, new_z, flow_x, flow_z, *fields[4:]]


def stress(fields, sides, coeffs, lane):
    vel_x, vel_z, flow_x, flow_z, xx, zz, xz, pressure = fields
    lame, shear, couple, fluid = coeffs
    strain_z = depth_upper(vel_z, lane)
    dilation = sides[0] + strain_z
    inflow = sides[2] + depth_upper(flow_z, lane)
    shared = lame * dilation - couple * inflow
    twice = 2.0 * shear
    xx = xx + shared + twice * sides[0]
    zz = zz + shared + twice * strain_z
    xz = xz + shear * (depth_upper(vel_x, lane) + sides[1])
    pressure = pressure - couple * dilation - fluid * inflow
    return [vel_x, vel_z, flow_x, flow_z, xx, zz, xz, pressure]


def side_share(row, coeffs):
    lame, shear, couple, fluid = coeffs
    zz = lame * row[0] - couple * row[2]
    pressure = -couple * row[0] - fluid * row[2]
    return [zz + 2.0 * shear * row[0], zz, shear * row[1], pressure]


def beyond_share(row, coeffs):
    xx, _, xz, pressure = side_share(row, coeffs)
    return [xx, xz, pressure]


def edge(fields):
    return [fields[XX], fields[XZ], fields[PR]]


def front(fields):
    return [fields[VX], fields[VZ], fields[QX]]


def minus(first, second):
    return [a - b for a, b in zip(first, second)]


def plus(first, second):
    return [a + b for a, b in zip(first, second)]


def kernel(
    n, scale, st_hbm, fw_hbm, vc_hbm, sc_hbm, cell_hbm, df_hbm, sid_hbm, out_ref, grad_ref,
    st, fw, vc_ref, sc_ref, cell_ref, df_ref, sid_ref, flat, tab, wide, keep, up, down, low, high, sums,
    st_sem, fw_sem, small_sem, up_sem, down_sem, sum_send, sum_recv,
):
    _, cells, depth = st.shape
    events = up.shape[1]
    rows = cells // events
    sources = df_ref.shape[0]
    me = lax.axis_index("gx")
    part = cells // CHUNKS
    smalls = [
        pltpu.make_async_copy(src, dst, small_sem.at[i])
        for i, (src, dst) in enumerate(
            [(df_hbm, df_ref), (cell_hbm, cell_ref), (sid_hbm, sid_ref), (vc_hbm, vc_ref), (sc_hbm, sc_ref)]
        )
    ]
    for small in smalls:
        small.start()
    loads = []
    for c in range(CHUNKS):
        at = pl.ds(c * part, part)
        loads.append(pltpu.make_async_copy(st_hbm.at[:, at], st.at[:, at], st_sem.at[c]))
        loads[-1].start()
    fw_load = pltpu.make_async_copy(fw_hbm, fw, fw_sem)
    fw_load.start()

    barrier = pltpu.get_barrier_semaphore()

    def greet(peer):
        pl.semaphore_signal(barrier, inc=1, device_id={"gx": peer}, device_id_type=pl.DeviceIdType.MESH)

    stages = []
    for stride, size in sum_stages(n):
        slot = lax.rem(me // stride, size)
        others = [lax.rem(slot + d, size) for d in range(1, size)]
        peers = [me + (other - slot) * stride for other in others]
        stages.append((slot, others, peers))
    for _, _, peers in stages:
        for peer in peers:
            greet(peer)

    @pl.when(me > 0)
    def _():
        greet(me - 1)

    @pl.when(me < n - 1)
    def _():
        greet(me + 1)

    greetings = sum(len(peers) for _, _, peers in stages)
    greetings = greetings + jnp.where(me > 0, 1, 0) + jnp.where(me < n - 1, 1, 0)

    for small in smalls:
        small.wait()
    vel = coeff_rows(vc_ref[...])
    coeffs = coeff_rows(sc_ref[...])

    force = jnp.concatenate([df_ref[:, t, c, :] for t in range(2) for c in range(2)], axis=0)
    first = force.astype(jnp.bfloat16)
    rest = force - first.astype(jnp.float32)
    second = rest.astype(jnp.bfloat16)
    third = (rest - second.astype(jnp.float32)).astype(jnp.bfloat16)
    pieces = jnp.concatenate([first, second, third], axis=0)
    count = force.shape[0]
    place = cell_ref[...] - me * (rows * depth)
    spot = lax.broadcasted_iota(jnp.int32, (depth, place.shape[1]), 0)
    planes = {}
    for x in range(rows):
        hot = jnp.where(spot + x * depth == place, 1.0, 0.0).astype(jnp.bfloat16)
        got = lax.dot_general(pieces, hot, (((1,), (1,)), ((), ())), preferred_element_type=jnp.float32)
        got = got[:count] + got[count : 2 * count] + got[2 * count :]
        flat[pl.ds(x, count, stride=rows), :] = got
        planes[x] = got
    tab[...] = flat[...].reshape(tab.shape)

    row_id = lax.broadcasted_iota(jnp.int32, (8, sources), 0)
    source_at = lax.broadcasted_iota(jnp.int32, (8, sources), 1)
    blocks = []
    for b in range(events // 8):
        wanted = jnp.full((8, sources), sid_ref[b * 8], jnp.int32)
        for r in range(1, 8):
            wanted = jnp.where(row_id == r, sid_ref[b * 8 + r], wanted)
        blocks.append(jnp.where(wanted == source_at, 1.0, 0.0))
    picked = jnp.concatenate(blocks, axis=0)

    def row_forcing(x, t):
        return [
            jnp.dot(
                picked, planes[x][(t * 2 + c) * sources : (t * 2 + c + 1) * sources],
                precision=lax.Precision.HIGHEST, preferred_element_type=jnp.float32,
            )
            for c in range(2)
        ]

    last = rows - 1
    slot_of = {0: 0, 1: 8, last: 16, last - 1: 24}
    force_0, force_1, force_last = row_forcing(0, 0), row_forcing(1, 0), row_forcing(last, 0)
    later_0 = row_forcing(0, 1)

    lane = lax.broadcasted_iota(jnp.int32, (8, depth), 1)
    at_row = lax.broadcasted_iota(jnp.int32, (rows, depth), 0)
    zero = jnp.zeros((8, depth), jnp.float32)
    blocks = range(events // 8)

    per_chunk = events // 8 // CHUNKS
    ups, downs = [], []
    for c in range(CHUNKS):
        some = pl.ds(c * per_chunk * 8, per_chunk * 8)
        ups.append(
            pltpu.make_async_remote_copy(
                up.at[:, some], low.at[:, some], up_sem.at[0, c], up_sem.at[1, c],
                device_id={"gx": jnp.minimum(me + 1, n - 1)}, device_id_type=pl.DeviceIdType.MESH,
            )
        )
        downs.append(
            pltpu.make_async_remote_copy(
                down.at[:, some], high.at[:, some], down_sem.at[0, c], down_sem.at[1, c],
                device_id={"gx": jnp.maximum(me - 1, 0)}, device_id_type=pl.DeviceIdType.MESH,
            )
        )

    for b in blocks:
        mine = slice(b * 8, (b + 1) * 8)
        c = b // per_chunk
        if b % per_chunk == 0:
            loads[c].wait()

        def row(x, names=range(8)):
            return [st[f, pl.ds(b * 8 * rows + x, 8, stride=rows), :] for f in names]

        row_last = row(last)
        sides = minus(edge(row_last), row(last - 1, (XX, XZ, PR)))
        one_last = velocity(row_last, sides, vel, lane, [v[mine] for v in force_last])
        one_last = stress(one_last, [-v for v in front(one_last)], coeffs, lane)
        for i, v in enumerate(edge(row_last) + edge(one_last)):
            up[i, mine, :] = v
        row_0, row_1 = row(0), row(1)
        one_0 = velocity(row_0, edge(row_0), vel, lane, [v[mine] for v in force_0])
        sides = minus(edge(row_1), edge(row_0))
        one_1 = velocity(row_1, sides, vel, lane, [v[mine] for v in force_1])
        two_0 = stress(one_0, minus(front(one_1), front(one_0)), coeffs, lane)
        two_0 = velocity(two_0, edge(two_0), vel, lane, [v[mine] for v in later_0])
        for i, v in enumerate(front(one_0) + front(two_0)):
            down[i, mine, :] = v
        if b % per_chunk == per_chunk - 1:
            if c == 0:
                pl.semaphore_wait(barrier, greetings)
            pl.when(me < n - 1)(ups[c].start)
            pl.when(me > 0)(downs[c].start)

    fw_load.wait()

    def lower(values):
        return values - jnp.where(at_row == 0, 0.0, pltpu.roll(values, 1, 0))

    def upper(values):
        return jnp.where(at_row == last, 0.0, pltpu.roll(values, last, 0)) - values

    def pair(i, totals):
        perm, poro = totals
        both = pl.ds(pl.multiple_of(i * 2 * rows, 2 * rows), 2 * rows)
        stored = [fw[k, both, :].astype(jnp.float32) for k in range(6)]
        for k in range(6):
            wide[k, both, :] = stored[k]
        for half in range(2):
            e = i * 2 + half
            at = pl.ds(pl.multiple_of(e * rows, rows), rows)
            own = slice(half * rows, (half + 1) * rows)
            source = sid_ref[e]
            fields = [st[f, at, :] for f in range(8)]
            for t in range(2):
                forcing = [tab[(t * 2 + c) * sources + source] for c in range(2)]
                fields = velocity(fields, [lower(v) for v in edge(fields)], vel, lane, forcing)
                perm = perm + fields[QX] * stored[3 * t][own] + fields[QZ] * stored[3 * t + 1][own]
                fields = stress(fields, [upper(v) for v in front(fields)], coeffs, lane)
                poro = poro + fields[PR] * stored[3 * t + 2][own]
            for f in range(8):
                out_ref[f, at, :] = fields[f]
        return perm, poro

    perm, poro = lax.fori_loop(0, events // 2, pair, (zero, zero), unroll=4)

    @pl.when(me == 0)
    def _():
        low[...] = jnp.zeros(low.shape, jnp.float32)

    @pl.when(me == n - 1)
    def _():
        high[...] = jnp.zeros(high.shape, jnp.float32)

    has_low = jnp.where(me > 0, 1.0, 0.0)
    has_high = jnp.where(me < n - 1, 1.0, 0.0)

    for b in blocks:
        mine = slice(b * 8, (b + 1) * 8)
        if b % per_chunk == 0:
            pl.when(me > 0)(ups[b // per_chunk].wait_recv)
            pl.when(me < n - 1)(downs[b // per_chunk].wait_recv)

        def seen(k, x):
            return wide[k, pl.ds(b * 8 * rows + x, 8, stride=rows), :]

        def add(x, names, values):
            for f, v in zip(names, values):
                keep[slot_of[x] + f, mine, :] = v

        one = velocity([zero] * 8, [-low[i, mine, :] for i in range(3)], vel, lane)
        perm = perm + one[QX] * seen(0, 0) + one[QZ] * seen(1, 0)
        met = plus([down[i, mine, :] for i in range(3)], front(one))
        rim = [low[3 + i, mine, :] + v for i, v in enumerate(beyond_share(met, coeffs))]
        rim = [v * has_low for v in rim]
        two = stress(one, [-v for v in front(one)], coeffs, lane)
        poro = poro + two[PR] * seen(2, 0)
        next_two = velocity([zero] * 8, [-v for v in edge(two)], vel, lane)
        two = velocity(two, minus(edge(two), rim), vel, lane)
        perm = perm + two[QX] * seen(3, 0) + two[QZ] * seen(4, 0)
        perm = perm + next_two[QX] * seen(3, 1) + next_two[QZ] * seen(4, 1)
        two = stress(two, minus(front(next_two), front(two)), coeffs, lane)
        next_two = stress(next_two, [-v for v in front(next_two)], coeffs, lane)
        poro = poro + two[PR] * seen(5, 0) + next_two[PR] * seen(5, 1)
        add(0, range(8), two)
        add(1, range(8), next_two)

        edge_last = [up[i, mine, :] for i in range(3)]
        one = velocity([zero] * 8, [-v for v in edge_last], vel, lane)
        met = [(high[i, mine, :] + v) * has_high for i, v in enumerate(front(one))]
        own = [zero] * 4 + side_share(met, coeffs)
        poro = poro + own[PR] * seen(2, last)
        two = stress(one, [-v for v in front(one)], coeffs, lane)
        full = [up[3 + i, mine, :] + v for i, v in enumerate(edge(own))]
        two = velocity(two, minus(edge(two), full), vel, lane)
        met = [(high[3 + i, mine, :] + v) * has_high for i, v in enumerate(front(two))]
        own = velocity(own, edge(own), vel, lane)
        perm = perm + own[QX] * seen(3, last) + own[QZ] * seen(4, last)
        prior = side_share(front(own), coeffs)
        own = stress(own, minus(met, front(own)), coeffs, lane)
        poro = poro + own[PR] * seen(5, last) + prior[3] * seen(5, last - 1)
        add(last, range(8), own)
        add(last - 1, range(XX, 8), prior)

    totals = (perm, poro)
    mine = jnp.concatenate([jnp.sum(total, axis=0, keepdims=True) for total in totals], axis=0)
    rest = [(b, x) for b in blocks for x in (0, 1, last, last - 1)]
    share = -(-len(rest) // len(stages))
    for i, (slot, others, peers) in enumerate(stages):
        buffer, send, recv = sums[i], sum_send[i], sum_recv[i]
        buffer[slot] = mine
        for peer in peers:
            copy = pltpu.make_async_remote_copy(
                buffer.at[slot], buffer.at[slot], send, recv,
                device_id={"gx": peer}, device_id_type=pl.DeviceIdType.MESH,
            )
            copy.start()
        for b, x in rest[i * share : (i + 1) * share]:
            at = pl.ds(b * 8 * rows + x, 8, stride=rows)
            for f in range(XX if x == last - 1 else 0, 8):
                out_ref[f, at, :] = out_ref[f, at, :] + keep[slot_of[x] + f, b * 8 : (b + 1) * 8, :]
        pltpu.make_async_copy(buffer.at[pl.ds(1, len(peers))], buffer.at[pl.ds(0, len(peers))], recv).wait()
        mine = buffer[0]
        for j in range(1, len(others) + 1):
            mine = mine + buffer[j]
    grad_ref[0:1, :] = vel[2] * vel[3] * mine[0:1] * scale
    grad_ref[1:2, :] = coeffs[3] * mine[1:2] * scale
    for (_, _, peers), buffer, send in zip(stages, sums, sum_send):
        pltpu.make_async_copy(buffer.at[pl.ds(1, len(peers))], buffer.at[pl.ds(0, len(peers))], send).wait()
    for c in range(CHUNKS):
        pl.when(me < n - 1)(ups[c].wait_send)
        pl.when(me > 0)(downs[c].wait_send)


def shards(adjoint_state, forward_fields, vel_coeffs, stress_coeffs, drm_cells, drm_force, source_id):
    fields, events, rows, depth = adjoint_state.shape
    cells = events * rows
    n = lax.axis_size("gx")
    scale = (events * rows * n) ** (-0.5)
    hbm, vmem = pl.BlockSpec(memory_space=pltpu.HBM), pl.BlockSpec(memory_space=pltpu.VMEM)
    f32 = jnp.float32
    dma = pltpu.SemaphoreType.DMA
    out, gradients = pl.pallas_call(
        functools.partial(kernel, n, scale),
        out_shape=[
            pltpu.VMEM((fields, cells, depth), f32),
            pltpu.VMEM((2, depth), f32),
        ],
        in_specs=[hbm] * 7,
        out_specs=[vmem, vmem],
        scratch_shapes=[
            pltpu.VMEM((fields, cells, depth), f32),
            pltpu.VMEM((6, cells, depth), jnp.bfloat16),
            pltpu.VMEM(vel_coeffs.shape, f32),
            pltpu.VMEM(stress_coeffs.shape, f32),
            pltpu.VMEM((1, drm_cells.shape[0]), jnp.int32),
            pltpu.VMEM(drm_force.shape, f32),
            pltpu.SMEM(source_id.shape, jnp.int32),
            pltpu.VMEM((4 * drm_force.shape[0] * rows, depth), f32),
            pltpu.VMEM((4 * drm_force.shape[0], rows, depth), f32),
            pltpu.VMEM((6, cells, depth), f32),
            pltpu.VMEM((32, events, depth), f32),
            pltpu.VMEM((6, events, depth), f32),
            pltpu.VMEM((6, events, depth), f32),
            pltpu.VMEM((6, events, depth), f32),
            pltpu.VMEM((6, events, depth), f32),
            [pltpu.VMEM((size, 2, depth), f32) for _, size in sum_stages(n)],
            dma((CHUNKS,)),
            dma,
            dma((5,)),
            dma((2, CHUNKS)),
            dma((2, CHUNKS)),
            [dma for _ in sum_stages(n)],
            [dma for _ in sum_stages(n)],
        ],
        compiler_params=pltpu.CompilerParams(
            collective_id=0, has_side_effects=True
        ),
    )(
        adjoint_state.reshape(fields, cells, depth),
        forward_fields.reshape(6, cells, depth),
        vel_coeffs,
        stress_coeffs,
        drm_cells.reshape(1, -1),
        drm_force,
        source_id,
    )
    return out.reshape(adjoint_state.shape), gradients


def solution(mesh):
    in_specs = (
        P(None, "groups", "gx", None),
        P(None, None, "groups", "gx", None),
        P("groups", None),
        P("groups", None),
        P("gx"),
        P("groups", None, None, "gx"),
        P("groups"),
    )
    out_specs = (P(None, "groups", "gx", None), P("groups", None))
    return jax.shard_map(shards, mesh=mesh, in_specs=in_specs, out_specs=out_specs, check_vma=False)
```

profile of v0, /device:TPU:0, one launch (start us, length us, event | category | flops | bytes accessed | tf_op | source)
XLA Modules:
  0.0 16.7 jit_solution(11767405219173352950)
XLA Ops:
  0.6 14.4 %shard_map.86 = (f32[8,384,128]{2,1,0:T(8,128)S(1)}, f32[2,128]{1,0:T(2,128)S(1)}) custom-call(f32[8,384,128]{2,1,0:T(8,128)} %bitcast.5, bf16[6,384,128]{2,1,0:T(8,128)(2,1)} %bitcast.6, f32[4,128]{1,0:T(4,128)} %vc_hbm.1, f32[4,128]{1,0:T(4,128)} %sc_hbm.1, s32[1,256]{1,0:T(1,128)} %bitcast.7, f32[16,2,2,256]{3,2,1,0:T(2,128)} %df_hbm.1, s32[48]{0:T(128)} %sid_hbm.1), custom_call_target="tpu_custom_call" | custom-call | tf_op jit(solution)/shard_map/pallas_call | solution.py:371
  15.0 1.1 %copy.11 = f32[8,48,8,128]{3,2,1,0:T(8,128)} copy(f32[8,48,8,128]{3,2,1,0:T(8,128)S(1)} %bitcast.4) | data formatting | bytes 3145728
  16.2 0.6 %copy.12 = f32[2,128]{1,0:T(2,128)} copy(f32[2,128]{1,0:T(2,128)S(1)} %get-tuple-element.7) | data formatting | bytes 2048
where the time goes:
time: 16.9 us; the launch traced here: 16.7 us
  Pallas kernels  14.4 us (85%)
  local copies, waits for them, and re-layouts  1.71 us (10%)
  between operations  0.64 us (4%)
    pallas_call x1, Pallas kernels, shards(): pl.pallas_call(functools.partial(kernel, n, scale), out_shape=[pltpu.VMEM...  14.4 us
    unnamed x2, local copies, waits for them, and re-layouts  1.71 us

commit v1 on v0

--- a/solution.py
+++ b/solution.py
@@ -9,11 +9,6 @@
 
 CHUNKS = 2
 VX, VZ, QX, QZ, XX, ZZ, XZ, PR = range(8)
-
-
-def sum_stages(n):
-    near = 4 if n % 4 == 0 else 1
-    return [(1, n)]
 
 
 def coeff_rows(coeffs):
@@ -92,7 +87,7 @@
 def kernel(
     n, scale, st_hbm, fw_hbm, vc_hbm, sc_hbm, cell_hbm, df_hbm, sid_hbm, out_ref, grad_ref,
     st, fw, vc_ref, sc_ref, cell_ref, df_ref, sid_ref, flat, tab, wide, keep, up, down, low, high, sums,
-    st_sem, fw_sem, small_sem, up_sem, down_sem, sum_send, sum_recv,
+    st_sem, fw_sem, small_sem, up_sem, down_sem, sum_send, sum_recv, here,
 ):
     _, cells, depth = st.shape
     events = up.shape[1]
@@ -118,29 +113,14 @@
 
     barrier = pltpu.get_barrier_semaphore()
 
-    def greet(peer):
-        pl.semaphore_signal(barrier, inc=1, device_id={"gx": peer}, device_id_type=pl.DeviceIdType.MESH)
-
-    stages = []
-    for stride, size in sum_stages(n):
-        slot = lax.rem(me // stride, size)
-        others = [lax.rem(slot + d, size) for d in range(1, size)]
-        peers = [me + (other - slot) * stride for other in others]
-        stages.append((slot, others, peers))
-    for _, _, peers in stages:
-        for peer in peers:
-            greet(peer)
+    def greet(semaphore, peer):
+        pl.semaphore_signal(semaphore, inc=1, device_id={"gx": peer}, device_id_type=pl.DeviceIdType.MESH)
 
     @pl.when(me > 0)
     def _():
-        greet(me - 1)
-
-    @pl.when(me < n - 1)
-    def _():
-        greet(me + 1)
-
-    greetings = sum(len(peers) for _, _, peers in stages)
-    greetings = greetings + jnp.where(me > 0, 1, 0) + jnp.where(me < n - 1, 1, 0)
+        greet(barrier, me - 1)
+
+    lax.fori_loop(me + 1, n, lambda peer, _: greet(barrier, peer), None)
 
     for small in smalls:
         small.wait()
@@ -236,10 +216,11 @@
             down[i, mine, :] = v
         if b % per_chunk == per_chunk - 1:
             if c == 0:
-                pl.semaphore_wait(barrier, greetings)
+                pl.semaphore_wait(barrier, me + jnp.where(me < n - 1, 1, 0))
             pl.when(me < n - 1)(ups[c].start)
             pl.when(me > 0)(downs[c].start)
 
+    lax.fori_loop(0, me, lambda peer, _: greet(here, peer), None)
     fw_load.wait()
 
     def lower(values):
@@ -331,33 +312,44 @@
         add(last - 1, range(XX, 8), prior)
 
     totals = (perm, poro)
-    mine = jnp.concatenate([jnp.sum(total, axis=0, keepdims=True) for total in totals], axis=0)
-    rest = [(b, x) for b in blocks for x in (0, 1, last, last - 1)]
-    share = -(-len(rest) // len(stages))
-    for i, (slot, others, peers) in enumerate(stages):
-        buffer, send, recv = sums[i], sum_send[i], sum_recv[i]
-        buffer[slot] = mine
-        for peer in peers:
-            copy = pltpu.make_async_remote_copy(
-                buffer.at[slot], buffer.at[slot], send, recv,
+    sums[me] = jnp.concatenate([jnp.sum(total, axis=0, keepdims=True) for total in totals], axis=0)
+
+    @pl.when(me < n - 1)
+    def _():
+        pl.semaphore_wait(here, n - 1 - me)
+
+    def send(peer, _):
+        @pl.when(peer != me)
+        def _():
+            pltpu.make_async_remote_copy(
+                sums.at[me], sums.at[me], sum_send, sum_recv,
                 device_id={"gx": peer}, device_id_type=pl.DeviceIdType.MESH,
-            )
-            copy.start()
-        for b, x in rest[i * share : (i + 1) * share]:
+            ).start()
+
+    lax.fori_loop(0, n, send, None)
+    for b in blocks:
+        for x in (0, 1, last, last - 1):
             at = pl.ds(b * 8 * rows + x, 8, stride=rows)
             for f in range(XX if x == last - 1 else 0, 8):
                 out_ref[f, at, :] = out_ref[f, at, :] + keep[slot_of[x] + f, b * 8 : (b + 1) * 8, :]
-        pltpu.make_async_copy(buffer.at[pl.ds(1, len(peers))], buffer.at[pl.ds(0, len(peers))], recv).wait()
-        mine = buffer[0]
-        for j in range(1, len(others) + 1):
-            mine = mine + buffer[j]
+    pltpu.make_async_copy(sums.at[pl.ds(1, n - 1)], sums.at[pl.ds(0, n - 1)], sum_recv).wait()
+    mine = jnp.sum(sums[...], axis=0)
     grad_ref[0:1, :] = vel[2] * vel[3] * mine[0:1] * scale
     grad_ref[1:2, :] = coeffs[3] * mine[1:2] * scale
-    for (_, _, peers), buffer, send in zip(stages, sums, sum_send):
-        pltpu.make_async_copy(buffer.at[pl.ds(1, len(peers))], buffer.at[pl.ds(0, len(peers))], send).wait()
+    pltpu.make_async_copy(sums.at[pl.ds(1, n - 1)], sums.at[pl.ds(0, n - 1)], sum_send).wait()
     for c in range(CHUNKS):
         pl.when(me < n - 1)(ups[c].wait_send)
         pl.when(me > 0)(downs[c].wait_send)
+
+
+def write(out_ref, grad_ref, out_hbm, grad_hbm, sems):
+    fields = out_ref.shape[0]
+    copies = [pltpu.make_async_copy(out_ref.at[f], out_hbm.at[f], sems.at[f]) for f in range(fields)]
+    copies.append(pltpu.make_async_copy(grad_ref, grad_hbm, sems.at[fields]))
+    for copy in copies:
+        copy.start()
+    for copy in copies:
+        copy.wait()
 
 
 def shards(adjoint_state, forward_fields, vel_coeffs, stress_coeffs, drm_cells, drm_force, source_id):
@@ -392,14 +384,15 @@
             pltpu.VMEM((6, events, depth), f32),
             pltpu.VMEM((6, events, depth), f32),
             pltpu.VMEM((6, events, depth), f32),
-            [pltpu.VMEM((size, 2, depth), f32) for _, size in sum_stages(n)],
+            pltpu.VMEM((n, 2, depth), f32),
             dma((CHUNKS,)),
             dma,
             dma((5,)),
             dma((2, CHUNKS)),
             dma((2, CHUNKS)),
-            [dma for _ in sum_stages(n)],
-            [dma for _ in sum_stages(n)],
+            dma,
+            dma,
+            pltpu.SemaphoreType.REGULAR,
         ],
         compiler_params=pltpu.CompilerParams(
             collective_id=0, has_side_effects=True
@@ -413,6 +406,13 @@
         drm_force,
         source_id,
     )
+    out, gradients = pl.pallas_call(
+        write,
+        out_shape=[jax.ShapeDtypeStruct(out.shape, f32), jax.ShapeDtypeStruct(gradients.shape, f32)],
+        in_specs=[pl.BlockSpec(memory_space=pl.ANY)] * 2,
+        out_specs=[hbm, hbm],
+        scratch_shapes=[dma((fields + 1,))],
+    )(pltpu.with_memory_space_constraint(out, pltpu.VMEM), pltpu.with_memory_space_constraint(gradients, pltpu.VMEM))
     return out.reshape(adjoint_state.shape), gradients
 
 

time: 16.9 us -> 15.6 us (0.923)
  local copies, waits for them, and re-layouts: 1.71 us -> 0 us
  Pallas kernels: 14.4 us -> 14.8 us
    unnamed x2 -> x0, local copies, waits for them, and re-layouts: 1.71 us -> none
    pallas_call x0 -> x1, Pallas kernels: none -> 1.21 us  [shards(): pl.pallas_call(write, out_shape=[jax.ShapeDtypeStruct(out.shape, f32), ja...]
    pallas_call x1, Pallas kernels: 14.4 us -> 13.6 us  [shards(): pl.pallas_call(functools.partial(kernel, n, scale), out_shape=[pltpu.VMEM...]
where the time goes in v1:
time: 15.6 us; the launch traced here: 15.4 us
  Pallas kernels  14.8 us (95%)
  between operations  0.64 us (4%)
    pallas_call x1, Pallas kernels, shards(): pl.pallas_call(functools.partial(kernel, n, scale), out_shape=[pltpu.VMEM...  13.6 us
    pallas_call x1, Pallas kernels, shards(): pl.pallas_call(write, out_shape=[jax.ShapeDtypeStruct(out.shape, f32), ja...  1.21 us

profile of v1, /device:TPU:0, one launch (start us, length us, event | category | flops | bytes accessed | tf_op | source)
XLA Modules:
  0.0 15.4 jit_solution(6531385696966706536)
XLA Ops:
  0.6 13.6 %shard_map.86 = (f32[8,384,128]{2,1,0:T(8,128)S(1)}, f32[2,128]{1,0:T(2,128)S(1)}) custom-call(f32[8,384,128]{2,1,0:T(8,128)} %bitcast.4, bf16[6,384,128]{2,1,0:T(8,128)(2,1)} %bitcast.5, f32[4,128]{1,0:T(4,128)} %vc_hbm.1, f32[4,128]{1,0:T(4,128)} %sc_hbm.1, s32[1,256]{1,0:T(1,128)} %bitcast.6, f32[16,2,2,256]{3,2,1,0:T(2,128)} %df_hbm.1, s32[48]{0:T(128)} %sid_hbm.1), custom_call_target="tpu_custom_call" | custom-call | tf_op jit(solution)/shard_map/pallas_call | solution.py:363
  14.2 1.2 %shard_map.87 = (f32[8,384,128]{2,1,0:T(8,128)}, f32[2,128]{1,0:T(2,128)}) custom-call(f32[8,384,128]{2,1,0:T(8,128)S(1)} %get-tuple-element.6.out_ref, f32[2,128]{1,0:T(2,128)S(1)} %get-tuple-element.7.grad_ref), custom_call_target="tpu_custom_call" | custom-call | tf_op jit(solution)/shard_map/pallas_call | solution.py:409

commit v2 on v1

--- a/solution.py
+++ b/solution.py
@@ -7,7 +7,7 @@
 from jax.experimental.pallas import tpu as pltpu
 from jax.sharding import PartitionSpec as P
 
-CHUNKS = 2
+LAYER = 8
 VX, VZ, QX, QZ, XX, ZZ, XZ, PR = range(8)
 
 
@@ -68,6 +68,28 @@
     return [xx, xz, pressure]
 
 
+def velocity_share(row, vel):
+    solid, couple, fluid, _ = vel
+    xx, xz, pressure = row
+    return [-(solid * xx + couple * pressure), -solid * xz, couple * xx + fluid * pressure, couple * xz]
+
+
+def stress_share(moved, sides, coeffs, lane):
+    vel_x, vel_z, flow_x, flow_z = moved
+    lame, shear, couple, fluid = coeffs
+    strain_z = depth_upper(vel_z, lane)
+    dilation = sides[0] + strain_z
+    inflow = sides[2] + depth_upper(flow_z, lane)
+    shared = lame * dilation - couple * inflow
+    twice = 2.0 * shear
+    return [
+        shared + twice * sides[0],
+        shared + twice * strain_z,
+        shear * (depth_upper(vel_x, lane) + sides[1]),
+        -couple * dilation - fluid * inflow,
+    ]
+
+
 def edge(fields):
     return [fields[XX], fields[XZ], fields[PR]]
 
@@ -94,7 +116,19 @@
     rows = cells // events
     sources = df_ref.shape[0]
     me = lax.axis_index("gx")
-    part = cells // CHUNKS
+    barrier = pltpu.get_barrier_semaphore()
+
+    def greet(semaphore, peer):
+        pl.semaphore_signal(semaphore, inc=1, device_id={"gx": peer}, device_id_type=pl.DeviceIdType.MESH)
+
+    @pl.when(me > 0)
+    def _():
+        greet(barrier, me - 1)
+
+    @pl.when(me < n - 1)
+    def _():
+        greet(barrier, me + 1)
+
     smalls = [
         pltpu.make_async_copy(src, dst, small_sem.at[i])
         for i, (src, dst) in enumerate(
@@ -103,47 +137,51 @@
     ]
     for small in smalls:
         small.start()
-    loads = []
-    for c in range(CHUNKS):
-        at = pl.ds(c * part, part)
-        loads.append(pltpu.make_async_copy(st_hbm.at[:, at], st.at[:, at], st_sem.at[c]))
-        loads[-1].start()
+    last = rows - 1
+    from_hbm, to_vmem = st_hbm.reshape(8, events, rows, depth), st.reshape(8, events, rows, depth)
+    loads = [
+        pltpu.make_async_copy(from_hbm.at[:, :, at], to_vmem.at[:, :, at], st_sem.at[i])
+        for i, at in enumerate([pl.ds(0, 2), pl.ds(last - 1, 2), pl.ds(2, rows - 4)])
+    ]
+    for load in loads:
+        load.start()
     fw_load = pltpu.make_async_copy(fw_hbm, fw, fw_sem)
     fw_load.start()
-
-    barrier = pltpu.get_barrier_semaphore()
-
-    def greet(semaphore, peer):
-        pl.semaphore_signal(semaphore, inc=1, device_id={"gx": peer}, device_id_type=pl.DeviceIdType.MESH)
-
-    @pl.when(me > 0)
+    lax.fori_loop(me + 2, n, lambda peer, _: greet(barrier, peer), None)
+
+    @pl.when(me == 0)
     def _():
-        greet(barrier, me - 1)
-
-    lax.fori_loop(me + 1, n, lambda peer, _: greet(barrier, peer), None)
+        low[...] = jnp.zeros(low.shape, jnp.float32)
+
+    @pl.when(me == n - 1)
+    def _():
+        high[...] = jnp.zeros(high.shape, jnp.float32)
 
     for small in smalls:
         small.wait()
     vel = coeff_rows(vc_ref[...])
     coeffs = coeff_rows(sc_ref[...])
 
+    def three(values):
+        first = values.astype(jnp.bfloat16)
+        rest = values - first.astype(jnp.float32)
+        second = rest.astype(jnp.bfloat16)
+        return [first, second, (rest - second.astype(jnp.float32)).astype(jnp.bfloat16)]
+
     force = jnp.concatenate([df_ref[:, t, c, :] for t in range(2) for c in range(2)], axis=0)
-    first = force.astype(jnp.bfloat16)
-    rest = force - first.astype(jnp.float32)
-    second = rest.astype(jnp.bfloat16)
-    third = (rest - second.astype(jnp.float32)).astype(jnp.bfloat16)
-    pieces = jnp.concatenate([first, second, third], axis=0)
     count = force.shape[0]
     place = cell_ref[...] - me * (rows * depth)
-    spot = lax.broadcasted_iota(jnp.int32, (depth, place.shape[1]), 0)
-    planes = {}
-    for x in range(rows):
-        hot = jnp.where(spot + x * depth == place, 1.0, 0.0).astype(jnp.bfloat16)
-        got = lax.dot_general(pieces, hot, (((1,), (1,)), ((), ())), preferred_element_type=jnp.float32)
-        got = got[:count] + got[count : 2 * count] + got[2 * count :]
-        flat[pl.ds(x, count, stride=rows), :] = got
-        planes[x] = got
-    tab[...] = flat[...].reshape(tab.shape)
+    column = lax.broadcasted_iota(jnp.int32, (depth, place.shape[1]), 0)
+    spot = (column // LAYER) * depth + (depth - LAYER) + lax.rem(column, LAYER)
+    hot = jnp.where(spot == place, 1.0, 0.0).astype(jnp.bfloat16)
+    got = lax.dot_general(
+        jnp.concatenate(three(force), axis=0), hot, (((1,), (1,)), ((), ())), preferred_element_type=jnp.float32
+    )
+    got = got[:count] + got[count : 2 * count] + got[2 * count :]
+
+    def placed(values, x):
+        at = lax.broadcasted_iota(jnp.int32, values.shape, 1)
+        return jnp.where(at < depth - LAYER, 0.0, pltpu.roll(values, depth - LAYER - x * LAYER, 1))
 
     row_id = lax.broadcasted_iota(jnp.int32, (8, sources), 0)
     source_at = lax.broadcasted_iota(jnp.int32, (8, sources), 1)
@@ -153,73 +191,90 @@
         for r in range(1, 8):
             wanted = jnp.where(row_id == r, sid_ref[b * 8 + r], wanted)
         blocks.append(jnp.where(wanted == source_at, 1.0, 0.0))
-    picked = jnp.concatenate(blocks, axis=0)
-
-    def row_forcing(x, t):
+    picked = jnp.concatenate(blocks, axis=0).astype(jnp.bfloat16)
+    picked = jnp.concatenate([picked] * 3, axis=1)
+
+    def event_forcing(t):
         return [
             jnp.dot(
-                picked, planes[x][(t * 2 + c) * sources : (t * 2 + c + 1) * sources],
-                precision=lax.Precision.HIGHEST, preferred_element_type=jnp.float32,
+                picked, jnp.concatenate(three(got[(t * 2 + c) * sources : (t * 2 + c + 1) * sources]), axis=0),
+                preferred_element_type=jnp.float32,
             )
             for c in range(2)
         ]
 
-    last = rows - 1
     slot_of = {0: 0, 1: 8, last: 16, last - 1: 24}
-    force_0, force_1, force_last = row_forcing(0, 0), row_forcing(1, 0), row_forcing(last, 0)
-    later_0 = row_forcing(0, 1)
+    now, later = event_forcing(0), event_forcing(1)
+    force_0, force_1, force_last = [[placed(v, x) for v in now] for x in (0, 1, last)]
+    later_0 = [placed(v, 0) for v in later]
 
     lane = lax.broadcasted_iota(jnp.int32, (8, depth), 1)
     at_row = lax.broadcasted_iota(jnp.int32, (rows, depth), 0)
     zero = jnp.zeros((8, depth), jnp.float32)
     blocks = range(events // 8)
 
-    per_chunk = events // 8 // CHUNKS
     ups, downs = [], []
-    for c in range(CHUNKS):
-        some = pl.ds(c * per_chunk * 8, per_chunk * 8)
+    for c in range(2):
+        half = pl.ds(3 * c, 3)
         ups.append(
             pltpu.make_async_remote_copy(
-                up.at[:, some], low.at[:, some], up_sem.at[0, c], up_sem.at[1, c],
+                up.at[half], low.at[half], up_sem.at[0, c], up_sem.at[1, c],
                 device_id={"gx": jnp.minimum(me + 1, n - 1)}, device_id_type=pl.DeviceIdType.MESH,
             )
         )
+    for c, part in enumerate([pl.ds(0, 3), pl.ds(3, 1), pl.ds(4, 2)]):
         downs.append(
             pltpu.make_async_remote_copy(
-                down.at[:, some], high.at[:, some], down_sem.at[0, c], down_sem.at[1, c],
+                down.at[part], high.at[part], down_sem.at[0, c], down_sem.at[1, c],
                 device_id={"gx": jnp.maximum(me - 1, 0)}, device_id_type=pl.DeviceIdType.MESH,
             )
         )
 
-    for b in blocks:
-        mine = slice(b * 8, (b + 1) * 8)
-        c = b // per_chunk
-        if b % per_chunk == 0:
-            loads[c].wait()
-
-        def row(x, names=range(8)):
-            return [st[f, pl.ds(b * 8 * rows + x, 8, stride=rows), :] for f in names]
-
-        row_last = row(last)
-        sides = minus(edge(row_last), row(last - 1, (XX, XZ, PR)))
+    def own_block(b):
+        return slice(b * 8, (b + 1) * 8)
+
+    def row(b, x, names=range(8)):
+        return [st[f, pl.ds(b * 8 * rows + x, 8, stride=rows), :] for f in names]
+
+    loads[0].wait()
+    firsts = []
+    for b in blocks:
+        row_0 = row(b, 0)
+        one_0 = velocity(row_0, edge(row_0), vel, lane, [v[own_block(b)] for v in force_0])
+        for i, v in enumerate(front(one_0)):
+            down[i, own_block(b), :] = v
+        firsts.append(one_0)
+    pl.semaphore_wait(barrier, me + jnp.where(me < n - 1, 1, 0))
+    pl.when(me > 0)(downs[0].start)
+    loads[1].wait()
+    for b in blocks:
+        for i, v in enumerate(row(b, last, (XX, XZ, PR))):
+            up[i, own_block(b), :] = v
+    pl.when(me < n - 1)(ups[0].start)
+    for b in blocks:
+        mine = own_block(b)
+        row_0, row_1, one_0 = row(b, 0, (XX, XZ, PR)), row(b, 1), firsts[b]
+        one_1 = velocity(row_1, minus(edge(row_1), row_0), vel, lane, [v[mine] for v in force_1])
+        two_0 = stress(one_0, minus(front(one_1), front(one_0)), coeffs, lane)
+        two_0 = velocity(two_0, edge(two_0), vel, lane, [v[mine] for v in later_0])
+        down[3, mine, :] = coeffs[2] * two_0[VX] + coeffs[3] * two_0[QX]
+        down[4, mine, :] = two_0[VX]
+        down[5, mine, :] = two_0[VZ]
+    pl.when(me > 0)(downs[1].start)
+    for b in blocks:
+        mine = own_block(b)
+        row_last = row(b, last)
+        sides = minus(edge(row_last), row(b, last - 1, (XX, XZ, PR)))
         one_last = velocity(row_last, sides, vel, lane, [v[mine] for v in force_last])
         one_last = stress(one_last, [-v for v in front(one_last)], coeffs, lane)
-        for i, v in enumerate(edge(row_last) + edge(one_last)):
-            up[i, mine, :] = v
-        row_0, row_1 = row(0), row(1)
-        one_0 = velocity(row_0, edge(row_0), vel, lane, [v[mine] for v in force_0])
-        sides = minus(edge(row_1), edge(row_0))
-        one_1 = velocity(row_1, sides, vel, lane, [v[mine] for v in force_1])
-        two_0 = stress(one_0, minus(front(one_1), front(one_0)), coeffs, lane)
-        two_0 = velocity(two_0, edge(two_0), vel, lane, [v[mine] for v in later_0])
-        for i, v in enumerate(front(one_0) + front(two_0)):
-            down[i, mine, :] = v
-        if b % per_chunk == per_chunk - 1:
-            if c == 0:
-                pl.semaphore_wait(barrier, me + jnp.where(me < n - 1, 1, 0))
-            pl.when(me < n - 1)(ups[c].start)
-            pl.when(me > 0)(downs[c].start)
-
+        for i, v in enumerate(edge(one_last)):
+            up[3 + i, mine, :] = v
+    pl.when(me < n - 1)(ups[1].start)
+
+    for x in range(rows):
+        flat[pl.ds(x, count, stride=rows), :] = placed(got, x)
+    tab[...] = flat[...].reshape(tab.shape)
+    loads[2].wait()
     lax.fori_loop(0, me, lambda peer, _: greet(here, peer), None)
     fw_load.wait()
 
@@ -251,65 +306,66 @@
                 out_ref[f, at, :] = fields[f]
         return perm, poro
 
-    perm, poro = lax.fori_loop(0, events // 2, pair, (zero, zero), unroll=4)
-
-    @pl.when(me == 0)
-    def _():
-        low[...] = jnp.zeros(low.shape, jnp.float32)
-
-    @pl.when(me == n - 1)
-    def _():
-        high[...] = jnp.zeros(high.shape, jnp.float32)
-
+    perm, poro = lax.fori_loop(0, events // 2, pair, (zero, zero), unroll=12)
+
+    pl.when(me > 0)(downs[2].start)
     has_low = jnp.where(me > 0, 1.0, 0.0)
     has_high = jnp.where(me < n - 1, 1.0, 0.0)
 
-    for b in blocks:
-        mine = slice(b * 8, (b + 1) * 8)
-        if b % per_chunk == 0:
-            pl.when(me > 0)(ups[b // per_chunk].wait_recv)
-            pl.when(me < n - 1)(downs[b // per_chunk].wait_recv)
-
-        def seen(k, x):
-            return wide[k, pl.ds(b * 8 * rows + x, 8, stride=rows), :]
-
-        def add(x, names, values):
-            for f, v in zip(names, values):
-                keep[slot_of[x] + f, mine, :] = v
-
-        one = velocity([zero] * 8, [-low[i, mine, :] for i in range(3)], vel, lane)
-        perm = perm + one[QX] * seen(0, 0) + one[QZ] * seen(1, 0)
+    def seen(b, k, x):
+        return wide[k, pl.ds(b * 8 * rows + x, 8, stride=rows), :]
+
+    def add(b, x, names, values):
+        for f, v in zip(names, values):
+            keep[slot_of[x] + f, own_block(b), :] = v
+
+    pl.when(me > 0)(ups[0].wait_recv)
+    pl.when(me < n - 1)(downs[0].wait_recv)
+    for b in blocks:
+        mine = own_block(b)
+        one = velocity_share([low[i, mine, :] for i in range(3)], vel)
+        perm = perm + one[QX] * seen(b, 0, 0) + one[QZ] * seen(b, 1, 0)
         met = plus([down[i, mine, :] for i in range(3)], front(one))
-        rim = [low[3 + i, mine, :] + v for i, v in enumerate(beyond_share(met, coeffs))]
-        rim = [v * has_low for v in rim]
-        two = stress(one, [-v for v in front(one)], coeffs, lane)
-        poro = poro + two[PR] * seen(2, 0)
-        next_two = velocity([zero] * 8, [-v for v in edge(two)], vel, lane)
+        rim = [v * has_low for v in beyond_share(met, coeffs)]
+        two = one + stress_share(one, [-v for v in front(one)], coeffs, lane)
+        poro = poro + two[PR] * seen(b, 2, 0)
+        next_one = velocity_share(edge(two), vel)
+        perm = perm + next_one[QX] * seen(b, 3, 1) + next_one[QZ] * seen(b, 4, 1)
+        next_stress = stress_share(next_one, [-v for v in front(next_one)], coeffs, lane)
+        poro = poro + next_stress[3] * seen(b, 5, 1)
+        add(b, 1, range(8), next_one + next_stress)
         two = velocity(two, minus(edge(two), rim), vel, lane)
-        perm = perm + two[QX] * seen(3, 0) + two[QZ] * seen(4, 0)
-        perm = perm + next_two[QX] * seen(3, 1) + next_two[QZ] * seen(4, 1)
-        two = stress(two, minus(front(next_two), front(two)), coeffs, lane)
-        next_two = stress(next_two, [-v for v in front(next_two)], coeffs, lane)
-        poro = poro + two[PR] * seen(5, 0) + next_two[PR] * seen(5, 1)
-        add(0, range(8), two)
-        add(1, range(8), next_two)
-
-        edge_last = [up[i, mine, :] for i in range(3)]
-        one = velocity([zero] * 8, [-v for v in edge_last], vel, lane)
+        add(b, 0, range(8), two)
+
+        one = velocity_share([up[i, mine, :] for i in range(3)], vel)
         met = [(high[i, mine, :] + v) * has_high for i, v in enumerate(front(one))]
-        own = [zero] * 4 + side_share(met, coeffs)
-        poro = poro + own[PR] * seen(2, last)
-        two = stress(one, [-v for v in front(one)], coeffs, lane)
-        full = [up[3 + i, mine, :] + v for i, v in enumerate(edge(own))]
+        own_stress = side_share(met, coeffs)
+        poro = poro + own_stress[3] * seen(b, 2, last)
+        two = one + stress_share(one, [-v for v in front(one)], coeffs, lane)
+        full = plus([up[3 + i, mine, :] for i in range(3)], [own_stress[0], own_stress[2], own_stress[3]])
         two = velocity(two, minus(edge(two), full), vel, lane)
-        met = [(high[3 + i, mine, :] + v) * has_high for i, v in enumerate(front(two))]
-        own = velocity(own, edge(own), vel, lane)
-        perm = perm + own[QX] * seen(3, last) + own[QZ] * seen(4, last)
+        beyond = [v * has_high for v in front(two)]
+        own = velocity([zero] * 4 + own_stress, [own_stress[0], own_stress[2], own_stress[3]], vel, lane)
+        perm = perm + own[QX] * seen(b, 3, last) + own[QZ] * seen(b, 4, last)
         prior = side_share(front(own), coeffs)
-        own = stress(own, minus(met, front(own)), coeffs, lane)
-        poro = poro + own[PR] * seen(5, last) + prior[3] * seen(5, last - 1)
-        add(last, range(8), own)
-        add(last - 1, range(XX, 8), prior)
+        own = stress(own, minus(beyond, front(own)), coeffs, lane)
+        poro = poro + own[PR] * seen(b, 5, last) + prior[3] * seen(b, 5, last - 1)
+        add(b, last, range(8), own)
+        add(b, last - 1, range(XX, 8), prior)
+
+    pl.when(me > 0)(ups[1].wait_recv)
+    pl.when(me < n - 1)(downs[1].wait_recv)
+    for b in blocks:
+        mine = own_block(b)
+        late = velocity_share([low[3 + i, mine, :] for i in range(3)], vel)
+        two = [keep[slot_of[0] + f, mine, :] for f in range(8)]
+        two = plus(two[:4], late) + two[4:]
+        perm = perm + two[QX] * seen(b, 3, 0) + two[QZ] * seen(b, 4, 0)
+        after = [keep[slot_of[1] + f, mine, :] for f in (VX, VZ, QX)]
+        two = stress(two, minus(after, front(two)), coeffs, lane)
+        poro = poro + two[PR] * seen(b, 5, 0)
+        add(b, 0, range(8), two)
+        poro = poro - high[3, mine, :] * seen(b, 5, last)
 
     totals = (perm, poro)
     sums[me] = jnp.concatenate([jnp.sum(total, axis=0, keepdims=True) for total in totals], axis=0)
@@ -327,6 +383,13 @@
             ).start()
 
     lax.fori_loop(0, n, send, None)
+    pl.when(me < n - 1)(downs[2].wait_recv)
+    for b in blocks:
+        mine = own_block(b)
+        beyond_x, beyond_z = high[4, mine, :], high[5, mine, :]
+        beyond_flow = (high[3, mine, :] - coeffs[2] * beyond_x) / coeffs[3]
+        late = side_share([beyond_x, beyond_z, beyond_flow], coeffs)[:3] + [-high[3, mine, :]]
+        add(b, last, range(XX, 8), plus([keep[slot_of[last] + f, mine, :] for f in range(XX, 8)], late))
     for b in blocks:
         for x in (0, 1, last, last - 1):
             at = pl.ds(b * 8 * rows + x, 8, stride=rows)
@@ -337,9 +400,10 @@
     grad_ref[0:1, :] = vel[2] * vel[3] * mine[0:1] * scale
     grad_ref[1:2, :] = coeffs[3] * mine[1:2] * scale
     pltpu.make_async_copy(sums.at[pl.ds(1, n - 1)], sums.at[pl.ds(0, n - 1)], sum_send).wait()
-    for c in range(CHUNKS):
-        pl.when(me < n - 1)(ups[c].wait_send)
-        pl.when(me > 0)(downs[c].wait_send)
+    for copy in ups:
+        pl.when(me < n - 1)(copy.wait_send)
+    for copy in downs:
+        pl.when(me > 0)(copy.wait_send)
 
 
 def write(out_ref, grad_ref, out_hbm, grad_hbm, sems):
@@ -385,11 +449,11 @@
             pltpu.VMEM((6, events, depth), f32),
             pltpu.VMEM((6, events, depth), f32),
             pltpu.VMEM((n, 2, depth), f32),
-            dma((CHUNKS,)),
+            dma((3,)),
             dma,
             dma((5,)),
-            dma((2, CHUNKS)),
-            dma((2, CHUNKS)),
+            dma((2, 2)),
+            dma((2, 3)),
             dma,
             dma,
             pltpu.SemaphoreType.REGULAR,

time: 15.6 us -> 15 us (0.962)
  Pallas kernels: 14.8 us -> 14.2 us
    pallas_call x1, Pallas kernels: 13.6 us -> 13 us  [shards(): pl.pallas_call(functools.partial(kernel, n, scale), out_shape=[pltpu.VMEM...]
where the time goes in v2:
time: 15 us; the launch traced here: 14.8 us
  Pallas kernels  14.2 us (95%)
  between operations  0.64 us (4%)
    pallas_call x1, Pallas kernels, shards(): pl.pallas_call(functools.partial(kernel, n, scale), out_shape=[pltpu.VMEM...  13 us
    pallas_call x1, Pallas kernels, shards(): pl.pallas_call(write, out_shape=[jax.ShapeDtypeStruct(out.shape, f32), ja...  1.21 us

profile of v2, /device:TPU:0, one launch (start us, length us, event | category | flops | bytes accessed | tf_op | source)
XLA Modules:
  0.0 14.8 jit_solution(7629181284531725426)
XLA Ops:
  0.6 13.0 %shard_map.86 = (f32[8,384,128]{2,1,0:T(8,128)S(1)}, f32[2,128]{1,0:T(2,128)S(1)}) custom-call(f32[8,384,128]{2,1,0:T(8,128)} %bitcast.4, bf16[6,384,128]{2,1,0:T(8,128)(2,1)} %bitcast.5, f32[4,128]{1,0:T(4,128)} %vc_hbm.1, f32[4,128]{1,0:T(4,128)} %sc_hbm.1, s32[1,256]{1,0:T(1,128)} %bitcast.6, f32[16,2,2,256]{3,2,1,0:T(2,128)} %df_hbm.1, s32[48]{0:T(128)} %sid_hbm.1), custom_call_target="tpu_custom_call" | custom-call | tf_op jit(solution)/shard_map/pallas_call | solution.py:427
  13.6 1.2 %shard_map.87 = (f32[8,384,128]{2,1,0:T(8,128)}, f32[2,128]{1,0:T(2,128)}) custom-call(f32[8,384,128]{2,1,0:T(8,128)S(1)} %get-tuple-element.6.out_ref, f32[2,128]{1,0:T(2,128)S(1)} %get-tuple-element.7.grad_ref), custom_call_target="tpu_custom_call" | custom-call | tf_op jit(solution)/shard_map/pallas_call | solution.py:473

commit v3 on v2

--- a/solution.py
+++ b/solution.py
@@ -143,10 +143,9 @@
         pltpu.make_async_copy(from_hbm.at[:, :, at], to_vmem.at[:, :, at], st_sem.at[i])
         for i, at in enumerate([pl.ds(0, 2), pl.ds(last - 1, 2), pl.ds(2, rows - 4)])
     ]
-    for load in loads:
-        load.start()
+    loads[0].start()
+    loads[1].start()
     fw_load = pltpu.make_async_copy(fw_hbm, fw, fw_sem)
-    fw_load.start()
     lax.fori_loop(me + 2, n, lambda peer, _: greet(barrier, peer), None)
 
     @pl.when(me == 0)
@@ -237,6 +236,8 @@
         return [st[f, pl.ds(b * 8 * rows + x, 8, stride=rows), :] for f in names]
 
     loads[0].wait()
+    loads[2].start()
+    fw_load.start()
     firsts = []
     for b in blocks:
         row_0 = row(b, 0)

time: 15 us -> 14.7 us (0.980)
  Pallas kernels: 14.2 us -> 13.9 us
    pallas_call x1, Pallas kernels: 13 us -> 12.7 us  [shards(): pl.pallas_call(functools.partial(kernel, n, scale), out_shape=[pltpu.VMEM...]
where the time goes in v3:
time: 14.7 us; the launch traced here: 14.5 us
  Pallas kernels  13.9 us (95%)
  between operations  0.64 us (4%)
    pallas_call x1, Pallas kernels, shards(): pl.pallas_call(functools.partial(kernel, n, scale), out_shape=[pltpu.VMEM...  12.7 us
    pallas_call x1, Pallas kernels, shards(): pl.pallas_call(write, out_shape=[jax.ShapeDtypeStruct(out.shape, f32), ja...  1.21 us

profile of v3, /device:TPU:0, one launch (start us, length us, event | category | flops | bytes accessed | tf_op | source)
XLA Modules:
  0.0 14.5 jit_solution(14831605912961601124)
XLA Ops:
  0.6 12.7 %shard_map.86 = (f32[8,384,128]{2,1,0:T(8,128)S(1)}, f32[2,128]{1,0:T(2,128)S(1)}) custom-call(f32[8,384,128]{2,1,0:T(8,128)} %bitcast.4, bf16[6,384,128]{2,1,0:T(8,128)(2,1)} %bitcast.5, f32[4,128]{1,0:T(4,128)} %vc_hbm.1, f32[4,128]{1,0:T(4,128)} %sc_hbm.1, s32[1,256]{1,0:T(1,128)} %bitcast.6, f32[16,2,2,256]{3,2,1,0:T(2,128)} %df_hbm.1, s32[48]{0:T(128)} %sid_hbm.1), custom_call_target="tpu_custom_call" | custom-call | tf_op jit(solution)/shard_map/pallas_call | solution.py:428
  13.3 1.2 %shard_map.87 = (f32[8,384,128]{2,1,0:T(8,128)}, f32[2,128]{1,0:T(2,128)}) custom-call(f32[8,384,128]{2,1,0:T(8,128)S(1)} %get-tuple-element.6.out_ref, f32[2,128]{1,0:T(2,128)S(1)} %get-tuple-element.7.grad_ref), custom_call_target="tpu_custom_call" | custom-call | tf_op jit(solution)/shard_map/pallas_call | solution.py:474

commit v4 on v3

--- a/solution.py
+++ b/solution.py
@@ -107,7 +107,7 @@
 
 
 def kernel(
-    n, scale, st_hbm, fw_hbm, vc_hbm, sc_hbm, cell_hbm, df_hbm, sid_hbm, out_ref, grad_ref,
+    n, scale, st_hbm, fw_hbm, vc_hbm, sc_hbm, cell_hbm, df_hbm, sid_hbm, out_ref, sums_ref, factor_ref,
     st, fw, vc_ref, sc_ref, cell_ref, df_ref, sid_ref, flat, tab, wide, keep, up, down, low, high, sums,
     st_sem, fw_sem, small_sem, up_sem, down_sem, sum_send, sum_recv, here,
 ):
@@ -278,6 +278,8 @@
     loads[2].wait()
     lax.fori_loop(0, me, lambda peer, _: greet(here, peer), None)
     fw_load.wait()
+    factor_ref[0:1, :] = vel[2] * vel[3] * scale
+    factor_ref[1:2, :] = coeffs[3] * scale
 
     def lower(values):
         return values - jnp.where(at_row == 0, 0.0, pltpu.roll(values, 1, 0))
@@ -397,9 +399,7 @@
             for f in range(XX if x == last - 1 else 0, 8):
                 out_ref[f, at, :] = out_ref[f, at, :] + keep[slot_of[x] + f, b * 8 : (b + 1) * 8, :]
     pltpu.make_async_copy(sums.at[pl.ds(1, n - 1)], sums.at[pl.ds(0, n - 1)], sum_recv).wait()
-    mine = jnp.sum(sums[...], axis=0)
-    grad_ref[0:1, :] = vel[2] * vel[3] * mine[0:1] * scale
-    grad_ref[1:2, :] = coeffs[3] * mine[1:2] * scale
+    sums_ref[...] = sums[...]
     pltpu.make_async_copy(sums.at[pl.ds(1, n - 1)], sums.at[pl.ds(0, n - 1)], sum_send).wait()
     for copy in ups:
         pl.when(me < n - 1)(copy.wait_send)
@@ -407,12 +407,15 @@
         pl.when(me > 0)(copy.wait_send)
 
 
-def write(out_ref, grad_ref, out_hbm, grad_hbm, sems):
-    fields = out_ref.shape[0]
-    copies = [pltpu.make_async_copy(out_ref.at[f], out_hbm.at[f], sems.at[f]) for f in range(fields)]
-    copies.append(pltpu.make_async_copy(grad_ref, grad_hbm, sems.at[fields]))
+def write(out_ref, sums_ref, factor_ref, out_hbm, grad_hbm, grad, sems):
+    half = out_ref.shape[0] // 2
+    parts = [pl.ds(0, half), pl.ds(half, half)]
+    copies = [pltpu.make_async_copy(out_ref.at[at], out_hbm.at[at], sems.at[i]) for i, at in enumerate(parts)]
     for copy in copies:
         copy.start()
+    grad[...] = factor_ref[...] * jnp.sum(sums_ref[...], axis=0)
+    copies.append(pltpu.make_async_copy(grad, grad_hbm, sems.at[2]))
+    copies[2].start()
     for copy in copies:
         copy.wait()
 
@@ -425,14 +428,15 @@
     hbm, vmem = pl.BlockSpec(memory_space=pltpu.HBM), pl.BlockSpec(memory_space=pltpu.VMEM)
     f32 = jnp.float32
     dma = pltpu.SemaphoreType.DMA
-    out, gradients = pl.pallas_call(
+    out, sums, factor = pl.pallas_call(
         functools.partial(kernel, n, scale),
         out_shape=[
             pltpu.VMEM((fields, cells, depth), f32),
+            pltpu.VMEM((n, 2, depth), f32),
             pltpu.VMEM((2, depth), f32),
         ],
         in_specs=[hbm] * 7,
-        out_specs=[vmem, vmem],
+        out_specs=[vmem] * 3,
         scratch_shapes=[
             pltpu.VMEM((fields, cells, depth), f32),
             pltpu.VMEM((6, cells, depth), jnp.bfloat16),
@@ -471,13 +475,14 @@
         drm_force,
         source_id,
     )
+    held = [pltpu.with_memory_space_constraint(v, pltpu.VMEM) for v in (out, sums, factor)]
     out, gradients = pl.pallas_call(
         write,
-        out_shape=[jax.ShapeDtypeStruct(out.shape, f32), jax.ShapeDtypeStruct(gradients.shape, f32)],
-        in_specs=[pl.BlockSpec(memory_space=pl.ANY)] * 2,
+        out_shape=[jax.ShapeDtypeStruct(out.shape, f32), jax.ShapeDtypeStruct(vel_coeffs[:2].shape, f32)],
+        in_specs=[pl.BlockSpec(memory_space=pl.ANY), vmem, vmem],
         out_specs=[hbm, hbm],
-        scratch_shapes=[dma((fields + 1,))],
-    )(pltpu.with_memory_space_constraint(out, pltpu.VMEM), pltpu.with_memory_space_constraint(gradients, pltpu.VMEM))
+        scratch_shapes=[pltpu.VMEM((2, depth), f32), dma((3,))],
+    )(*held)
     return out.reshape(adjoint_state.shape), gradients
 
 

time: 14.7 us -> 14.6 us (level)
  no operation moved by 1% of the time
where the time goes in v4:
time: 14.6 us; the launch traced here: 14.5 us
  Pallas kernels  13.8 us (95%)
  between operations  0.64 us (4%)
    pallas_call x1, Pallas kernels, shards(): pl.pallas_call(functools.partial(kernel, n, scale), out_shape=[pltpu.VMEM...  12.6 us
    pallas_call x1, Pallas kernels, shards(): pl.pallas_call(write, out_shape=[jax.ShapeDtypeStruct(out.shape, f32), ja...  1.17 us

profile of v4, /device:TPU:0, one launch (start us, length us, event | category | flops | bytes accessed | tf_op | source)
XLA Modules:
  0.0 14.5 jit_solution(10188653136471368625)
XLA Ops:
  0.6 12.6 %shard_map.86 = (f32[8,384,128]{2,1,0:T(8,128)S(1)}, f32[16,2,128]{2,1,0:T(2,128)S(1)}, f32[2,128]{1,0:T(2,128)S(1)}) custom-call(f32[8,384,128]{2,1,0:T(8,128)} %bitcast.4, bf16[6,384,128]{2,1,0:T(8,128)(2,1)} %bitcast.5, f32[4,128]{1,0:T(4,128)} %vc_hbm.1, f32[4,128]{1,0:T(4,128)} %sc_hbm.1, s32[1,256]{1,0:T(1,128)} %bitcast.6, f32[16,2,2,256]{3,2,1,0:T(2,128)} %df_hbm.1, ...), custom_call_target="tpu_custom_call" | custom-call | tf_op jit(solution)/shard_map/pallas_call | solution.py:431
  13.3 1.2 %shard_map.87 = (f32[8,384,128]{2,1,0:T(8,128)}, f32[2,128]{1,0:T(2,128)}) custom-call(f32[8,384,128]{2,1,0:T(8,128)S(1)} %get-tuple-element.7.out_ref, f32[16,2,128]{2,1,0:T(2,128)S(1)} %get-tuple-element.8.sums_ref, f32[2,128]{1,0:T(2,128)S(1)} %get-tuple-element.9.factor_ref), custom_call_target="tpu_custom_call" | custom-call | tf_op jit(solution)/shard_map/pallas_call | solution.py:479

commit v5 on v4

--- a/solution.py
+++ b/solution.py
@@ -72,6 +72,20 @@
     solid, couple, fluid, _ = vel
     xx, xz, pressure = row
     return [-(solid * xx + couple * pressure), -solid * xz, couple * xx + fluid * pressure, couple * xz]
+
+
+def velocity_stress(pulled, vel, lane):
+    solid, couple, fluid, _ = vel
+    xx, zz, xz, pressure = pulled
+    force_x = xx + depth_lower(xz, lane)
+    force_z = xz + depth_lower(zz, lane)
+    push_z = depth_lower(pressure, lane)
+    return [
+        solid * force_x + couple * pressure,
+        solid * force_z + couple * push_z,
+        -couple * force_x - fluid * pressure,
+        -couple * force_z - fluid * push_z,
+    ]
 
 
 def stress_share(moved, sides, coeffs, lane):
@@ -322,8 +336,19 @@
         for f, v in zip(names, values):
             keep[slot_of[x] + f, own_block(b), :] = v
 
+    def sides_of(pulled):
+        return [pulled[0], pulled[2], pulled[3]]
+
+    def top(b, pulled, beyond, totals):
+        perm, poro = totals
+        moved = velocity_stress(pulled, vel, lane)
+        perm = perm + moved[QX] * seen(b, 3, last) + moved[QZ] * seen(b, 4, last)
+        prior = side_share(front(moved), coeffs)
+        change = plus(pulled, stress_share(moved, minus(beyond, front(moved)), coeffs, lane))
+        poro = poro + pulled[3] * seen(b, 2, last) + change[3] * seen(b, 5, last) + prior[3] * seen(b, 5, last - 1)
+        return moved + change, prior, (perm, poro)
+
     pl.when(me > 0)(ups[0].wait_recv)
-    pl.when(me < n - 1)(downs[0].wait_recv)
     for b in blocks:
         mine = own_block(b)
         one = velocity_share([low[i, mine, :] for i in range(3)], vel)
@@ -341,23 +366,24 @@
         add(b, 0, range(8), two)
 
         one = velocity_share([up[i, mine, :] for i in range(3)], vel)
-        met = [(high[i, mine, :] + v) * has_high for i, v in enumerate(front(one))]
-        own_stress = side_share(met, coeffs)
-        poro = poro + own_stress[3] * seen(b, 2, last)
+        pulled = [v * has_high for v in side_share(front(one), coeffs)]
         two = one + stress_share(one, [-v for v in front(one)], coeffs, lane)
-        full = plus([up[3 + i, mine, :] for i in range(3)], [own_stress[0], own_stress[2], own_stress[3]])
-        two = velocity(two, minus(edge(two), full), vel, lane)
-        beyond = [v * has_high for v in front(two)]
-        own = velocity([zero] * 4 + own_stress, [own_stress[0], own_stress[2], own_stress[3]], vel, lane)
-        perm = perm + own[QX] * seen(b, 3, last) + own[QZ] * seen(b, 4, last)
-        prior = side_share(front(own), coeffs)
-        own = stress(own, minus(beyond, front(own)), coeffs, lane)
-        poro = poro + own[PR] * seen(b, 5, last) + prior[3] * seen(b, 5, last - 1)
+        full = plus([up[3 + i, mine, :] for i in range(3)], sides_of(pulled))
+        beyond = [v * has_high for v in front(velocity(two, minus(edge(two), full), vel, lane))]
+        own, prior, (perm, poro) = top(b, pulled, beyond, (perm, poro))
         add(b, last, range(8), own)
         add(b, last - 1, range(XX, 8), prior)
 
+    pl.when(me < n - 1)(downs[0].wait_recv)
+    for b in blocks:
+        pulled = side_share([high[i, own_block(b), :] for i in range(3)], coeffs)
+        beyond = front(velocity_share(sides_of(pulled), vel))
+        own, prior, (perm, poro) = top(b, pulled, beyond, (perm, poro))
+        add(b, last, range(8), plus(own, [keep[slot_of[last] + f, own_block(b), :] for f in range(8)]))
+        more = [keep[slot_of[last - 1] + f, own_block(b), :] for f in range(XX, 8)]
+        add(b, last - 1, range(XX, 8), plus(prior, more))
+
     pl.when(me > 0)(ups[1].wait_recv)
-    pl.when(me < n - 1)(downs[1].wait_recv)
     for b in blocks:
         mine = own_block(b)
         late = velocity_share([low[3 + i, mine, :] for i in range(3)], vel)
@@ -368,7 +394,10 @@
         two = stress(two, minus(after, front(two)), coeffs, lane)
         poro = poro + two[PR] * seen(b, 5, 0)
         add(b, 0, range(8), two)
-        poro = poro - high[3, mine, :] * seen(b, 5, last)
+
+    pl.when(me < n - 1)(downs[1].wait_recv)
+    for b in blocks:
+        poro = poro - high[3, own_block(b), :] * seen(b, 5, last)
 
     totals = (perm, poro)
     sums[me] = jnp.concatenate([jnp.sum(total, axis=0, keepdims=True) for total in totals], axis=0)

time: 14.6 us -> 14.5 us (level)
  no operation moved by 1% of the time
where the time goes in v5:
time: 14.5 us; the launch traced here: 14.4 us
  Pallas kernels  13.7 us (94%)
  between operations  0.64 us (4%)
    pallas_call x1, Pallas kernels, shards(): pl.pallas_call(functools.partial(kernel, n, scale), out_shape=[pltpu.VMEM...  12.6 us
    pallas_call x1, Pallas kernels, shards(): pl.pallas_call(write, out_shape=[jax.ShapeDtypeStruct(out.shape, f32), ja...  1.17 us

profile of v5, /device:TPU:0, one launch (start us, length us, event | category | flops | bytes accessed | tf_op | source)
XLA Modules:
  0.0 14.4 jit_solution(4185545673594298692)
XLA Ops:
  0.6 12.6 %shard_map.86 = (f32[8,384,128]{2,1,0:T(8,128)S(1)}, f32[16,2,128]{2,1,0:T(2,128)S(1)}, f32[2,128]{1,0:T(2,128)S(1)}) custom-call(f32[8,384,128]{2,1,0:T(8,128)} %bitcast.4, bf16[6,384,128]{2,1,0:T(8,128)(2,1)} %bitcast.5, f32[4,128]{1,0:T(4,128)} %vc_hbm.1, f32[4,128]{1,0:T(4,128)} %sc_hbm.1, s32[1,256]{1,0:T(1,128)} %bitcast.6, f32[16,2,2,256]{3,2,1,0:T(2,128)} %df_hbm.1, ...), custom_call_target="tpu_custom_call" | custom-call | tf_op jit(solution)/shard_map/pallas_call | solution.py:460
  13.2 1.2 %shard_map.87 = (f32[8,384,128]{2,1,0:T(8,128)}, f32[2,128]{1,0:T(2,128)}) custom-call(f32[8,384,128]{2,1,0:T(8,128)S(1)} %get-tuple-element.7.out_ref, f32[16,2,128]{2,1,0:T(2,128)S(1)} %get-tuple-element.8.sums_ref, f32[2,128]{1,0:T(2,128)S(1)} %get-tuple-element.9.factor_ref), custom_call_target="tpu_custom_call" | custom-call | tf_op jit(solution)/shard_map/pallas_call | solution.py:508

commit v6 on v5

--- a/solution.py
+++ b/solution.py
@@ -323,7 +323,7 @@
                 out_ref[f, at, :] = fields[f]
         return perm, poro
 
-    perm, poro = lax.fori_loop(0, events // 2, pair, (zero, zero), unroll=12)
+    perm, poro = lax.fori_loop(0, events // 2, pair, (zero, zero), unroll=8)
 
     pl.when(me > 0)(downs[2].start)
     has_low = jnp.where(me > 0, 1.0, 0.0)

time: 14.5 us -> 14.5 us (level)
  no operation moved by 1% of the time
where the time goes in v6:
time: 14.5 us; the launch traced here: 14.4 us
  Pallas kernels  13.7 us (94%)
  between operations  0.64 us (4%)
    pallas_call x1, Pallas kernels, shards(): pl.pallas_call(functools.partial(kernel, n, scale), out_shape=[pltpu.VMEM...  12.6 us
    pallas_call x1, Pallas kernels, shards(): pl.pallas_call(write, out_shape=[jax.ShapeDtypeStruct(out.shape, f32), ja...  1.17 us

profile of v6, /device:TPU:0, one launch (start us, length us, event | category | flops | bytes accessed | tf_op | source)
XLA Modules:
  0.0 14.4 jit_solution(13008331774170118411)
XLA Ops:
  0.6 12.6 %shard_map.86 = (f32[8,384,128]{2,1,0:T(8,128)S(1)}, f32[16,2,128]{2,1,0:T(2,128)S(1)}, f32[2,128]{1,0:T(2,128)S(1)}) custom-call(f32[8,384,128]{2,1,0:T(8,128)} %bitcast.4, bf16[6,384,128]{2,1,0:T(8,128)(2,1)} %bitcast.5, f32[4,128]{1,0:T(4,128)} %vc_hbm.1, f32[4,128]{1,0:T(4,128)} %sc_hbm.1, s32[1,256]{1,0:T(1,128)} %bitcast.6, f32[16,2,2,256]{3,2,1,0:T(2,128)} %df_hbm.1, ...), custom_call_target="tpu_custom_call" | custom-call | tf_op jit(solution)/shard_map/pallas_call | solution.py:460
  13.2 1.2 %shard_map.87 = (f32[8,384,128]{2,1,0:T(8,128)}, f32[2,128]{1,0:T(2,128)}) custom-call(f32[8,384,128]{2,1,0:T(8,128)S(1)} %get-tuple-element.7.out_ref, f32[16,2,128]{2,1,0:T(2,128)S(1)} %get-tuple-element.8.sums_ref, f32[2,128]{1,0:T(2,128)S(1)} %get-tuple-element.9.factor_ref), custom_call_target="tpu_custom_call" | custom-call | tf_op jit(solution)/shard_map/pallas_call | solution.py:508

commit v7 on v6

--- a/solution.py
+++ b/solution.py
@@ -290,7 +290,6 @@
         flat[pl.ds(x, count, stride=rows), :] = placed(got, x)
     tab[...] = flat[...].reshape(tab.shape)
     loads[2].wait()
-    lax.fori_loop(0, me, lambda peer, _: greet(here, peer), None)
     fw_load.wait()
     factor_ref[0:1, :] = vel[2] * vel[3] * scale
     factor_ref[1:2, :] = coeffs[3] * scale
@@ -326,6 +325,7 @@
     perm, poro = lax.fori_loop(0, events // 2, pair, (zero, zero), unroll=8)
 
     pl.when(me > 0)(downs[2].start)
+    lax.fori_loop(0, me, lambda peer, _: greet(here, peer), None)
     has_low = jnp.where(me > 0, 1.0, 0.0)
     has_high = jnp.where(me < n - 1, 1.0, 0.0)
 

time: 14.5 us -> 14.7 us (1.014)
  Pallas kernels: 13.7 us -> 13.9 us
    pallas_call x1, Pallas kernels: 12.6 us -> 12.7 us  [shards(): pl.pallas_call(functools.partial(kernel, n, scale), out_shape=[pltpu.VMEM...]
where the time goes in v7:
time: 14.7 us; the launch traced here: 14.5 us
  Pallas kernels  13.9 us (95%)
  between operations  0.64 us (4%)
    pallas_call x1, Pallas kernels, shards(): pl.pallas_call(functools.partial(kernel, n, scale), out_shape=[pltpu.VMEM...  12.7 us
    pallas_call x1, Pallas kernels, shards(): pl.pallas_call(write, out_shape=[jax.ShapeDtypeStruct(out.shape, f32), ja...  1.17 us

profile of v7, /device:TPU:0, one launch (start us, length us, event | category | flops | bytes accessed | tf_op | source)
XLA Modules:
  0.0 14.5 jit_solution(10966687678190804672)
XLA Ops:
  0.6 12.7 %shard_map.86 = (f32[8,384,128]{2,1,0:T(8,128)S(1)}, f32[16,2,128]{2,1,0:T(2,128)S(1)}, f32[2,128]{1,0:T(2,128)S(1)}) custom-call(f32[8,384,128]{2,1,0:T(8,128)} %bitcast.4, bf16[6,384,128]{2,1,0:T(8,128)(2,1)} %bitcast.5, f32[4,128]{1,0:T(4,128)} %vc_hbm.1, f32[4,128]{1,0:T(4,128)} %sc_hbm.1, s32[1,256]{1,0:T(1,128)} %bitcast.6, f32[16,2,2,256]{3,2,1,0:T(2,128)} %df_hbm.1, ...), custom_call_target="tpu_custom_call" | custom-call | tf_op jit(solution)/shard_map/pallas_call | solution.py:460
  13.4 1.2 %shard_map.87 = (f32[8,384,128]{2,1,0:T(8,128)}, f32[2,128]{1,0:T(2,128)}) custom-call(f32[8,384,128]{2,1,0:T(8,128)S(1)} %get-tuple-element.7.out_ref, f32[16,2,128]{2,1,0:T(2,128)S(1)} %get-tuple-element.8.sums_ref, f32[2,128]{1,0:T(2,128)S(1)} %get-tuple-element.9.factor_ref), custom_call_target="tpu_custom_call" | custom-call | tf_op jit(solution)/shard_map/pallas_call | solution.py:508
